TPU v7x, 512 devices: a whole 4x4x16 slice. The times are simulated.
512 devices in a mesh: grp: 64 (over z, x_lo, core), freq: 8 (over y, x_hi).
Axes of the slice: x: 4 (x_hi: 2, x_lo: 2; x = x_hi * 2 + x_lo), y: 4, z: 16, core: 2. Of those that a mesh axis runs over, the one named last changes fastest.
Arguments:
- spectra: bfloat16 [8192, 8, 2, 1024], P('grp', None, None, 'freq')
- pairing: int32 [2, 64], replicated, may hold values from 0 to 63, as said below
Outputs:
- correlations: float32 [2, 4096, 128, 256], P(None, ('grp', 'freq'))
Inputs may be any that keep to these rules, and one draw needn't show every extreme that they name: In every round each group's partner is another group, and pairing[r, pairing[r, g]] = g.
All inputs are finite; a program needn't handle non-finite values.
Results may differ from a plain program's by a relative error of at most 0.0055.
Values may be sent and summed in bfloat16 or wider, within the bound.
A program may use at most 64 MiB of HBM per device.

v0:
```python
import math

import jax
import jax.numpy as jnp
from jax import lax
from jax.sharding import PartitionSpec as P

LAGS = 256
VIRTUAL_SOURCES = 64
ROUNDS = 2


def lag_table(bin_count, freq_total):
    bins = jnp.arange(bin_count, dtype=jnp.int32)
    shifts = jnp.arange(LAGS, dtype=jnp.int32) - LAGS // 2
    phase_int = bins[:, None] * shifts[None, :] % (2 * freq_total)
    theta = phase_int.astype(jnp.float32) * (math.pi / freq_total)
    weights = jnp.where(bins == 0, 1.0, 2.0).astype(jnp.float32) / (2.0 * freq_total)
    return jnp.stack(
        [weights[:, None] * jnp.cos(theta), -weights[:, None] * jnp.sin(theta)]
    ).astype(jnp.bfloat16)


def cross_spectra(source_channels, partner):
    src_count, win_count, two_parts, bins = source_channels.shape
    real_left = source_channels.reshape(src_count, win_count * 2, bins)
    imag_left = jnp.stack([source_channels[:, :, 1], -source_channels[:, :, 0]], axis=2).reshape(
        src_count, win_count * 2, bins
    )
    right = partner.reshape(partner.shape[0], win_count * 2, bins)
    real_part = (
        jnp.einsum("skf,ckf->scf", real_left, right, preferred_element_type=jnp.float32) / win_count
    ).astype(jnp.bfloat16)
    imag_part = (
        jnp.einsum("skf,ckf->scf", imag_left, right, preferred_element_type=jnp.float32) / win_count
    ).astype(jnp.bfloat16)
    return jnp.stack([real_part, imag_part], axis=2)


def per_device(spectra, pairing):
    channel_total, win_count, two_parts, freq_local = spectra.shape
    freq_total = freq_local * lax.axis_size("freq")
    group_count = lax.axis_size("grp")
    per_slot = channel_total // group_count
    energy = lax.psum(jnp.sum(jnp.square(spectra.astype(jnp.float32)), axis=(1, 2, 3)), "freq")
    scaling = lax.rsqrt(energy / (win_count * 2 * freq_total) + 1e-06)
    whitened_spectra = (spectra * scaling[:, None, None, None]).astype(jnp.bfloat16)
    spread = lax.all_to_all(
        whitened_spectra.reshape(group_count, per_slot, win_count, two_parts, freq_local),
        "grp",
        split_axis=0,
        concat_axis=0,
        tiled=True,
    )
    source_channels = whitened_spectra[:: channel_total // VIRTUAL_SOURCES]
    shape_back = (channel_total, win_count, two_parts, freq_local)
    partners = []
    for which_round in range(ROUNDS):
        slots = jnp.take(spread, pairing[which_round], axis=0)
        arrived = lax.all_to_all(slots, "grp", split_axis=0, concat_axis=0, tiled=True)
        partners.append(arrived.reshape(shape_back))
    whole_table = lag_table(freq_total, freq_total)
    results = []
    for which_round in range(ROUNDS):
        spectrum = cross_spectra(source_channels, partners[which_round])
        results.append(
            jnp.einsum(
                "scpf,pfl->scl",
                lax.all_to_all(spectrum, "freq", split_axis=0, concat_axis=3, tiled=True),
                whole_table,
                preferred_element_type=jnp.float32,
            )
        )
    return jnp.stack(results)


def solution(mesh):
    placed = (P("grp", None, None, "freq"), P())
    return jax.shard_map(
        per_device,
        mesh=mesh,
        in_specs=placed,
        out_specs=P(None, ("grp", "freq"), None, None),
        check_vma=False,
    )
```

profile of v0, /device:TPU:32, one launch (start us, length us, event | category | flops | bytes accessed | tf_op | source)
XLA Modules:
  0.0 286.4 jit_solution(10637405546343010891)
XLA Ops:
  0.0 2.1 fusion.4
  2.1 24.5 %psum.7 = f32[128]{0:T(128)S(1)} all-reduce(f32[128]{0:T(128)S(1)} %fusion.4), channel_id=1, replica_groups=mesh['grp'=64,'freq'=8] {'freq'}, use_global_device_ids=true, to_apply=%region_1.0 | all-reduce | flops 128 | bytes 1024 | tf_op jit(solution)/shard_map/psum | solution.py:45
  26.6 1.5 fusion.5
  28.1 0.9 copy.18
  29.0 15.8 %all-to-all-start = ((bf16[64,2,8,2,128]{4,2,3,1,0:T(8,128)(2,1)}), bf16[64,2,8,2,128]{4,2,3,1,0:T(8,128)(2,1)S(1)}, u32[]{:S(2)}, u32[]{:S(2)}) async-start(bf16[64,2,8,2,128]{4,2,3,1,0:T(8,128)(2,1)} %bitcast.1), calls=%async_computation | async-start | bytes 1048576 | tf_op jit(solution)/shard_map/all_to_all | solution.py:48
  44.8 0.8 compare_and_fusion.1
  45.6 31.9 %all-to-all-done = bf16[64,2,8,2,128]{4,2,3,1,0:T(8,128)(2,1)S(1)} async-done(((bf16[64,2,8,2,128]{4,2,3,1,0:T(8,128)(2,1)}), bf16[64,2,8,2,128]{4,2,3,1,0:T(8,128)(2,1)S(1)}, u32[]{:S(2)}, u32[]{:S(2)}) %all-to-all-start) | async-done | bytes 524320 | tf_op jit(solution)/shard_map/all_to_all | solution.py:48
  78.1 0.9 broadcast_select_fusion.1
  79.0 5.6 %all-to-all-start.1 = ((bf16[64,2,8,2,128]{4,2,3,1,0:T(8,128)(2,1)}), bf16[64,2,8,2,128]{4,2,3,1,0:T(8,128)(2,1)S(1)}, u32[]{:S(2)}, u32[]{:S(2)}) async-start(bf16[64,2,8,2,128]{4,2,3,1,0:T(8,128)(2,1)} %broadcast_select_fusion.1), calls=%async_computation.1 | async-start | bytes 1048576 | tf_op jit(solution)/shard_map/all_to_all | solution.py:60
  85.3 0.9 broadcast_select_fusion
  86.2 31.1 %all-to-all-done.1 = bf16[64,2,8,2,128]{4,2,3,1,0:T(8,128)(2,1)S(1)} async-done(((bf16[64,2,8,2,128]{4,2,3,1,0:T(8,128)(2,1)}), bf16[64,2,8,2,128]{4,2,3,1,0:T(8,128)(2,1)S(1)}, u32[]{:S(2)}, u32[]{:S(2)}) %all-to-all-start.1) | async-done | bytes 524320 | tf_op jit(solution)/shard_map/all_to_all | solution.py:60
  117.3 5.6 %all-to-all-start.3 = ((bf16[64,2,8,2,128]{4,2,3,1,0:T(8,128)(2,1)}), bf16[64,2,8,2,128]{4,2,3,1,0:T(8,128)(2,1)S(1)}, u32[]{:S(2)}, u32[]{:S(2)}) async-start(bf16[64,2,8,2,128]{4,2,3,1,0:T(8,128)(2,1)} %broadcast_select_fusion), calls=%async_computation.3 | async-start | bytes 1048576 | tf_op jit(solution)/shard_map/all_to_all | solution.py:60
  125.8 0.7 copy.21
  126.5 0.8 fusion.1
  127.3 0.8 fusion
  128.5 4.6 %copy.24 = bf16[64,128,2,128]{1,3,2,0:T(8,128)(2,1)} copy(bf16[64,128,2,128]{1,0,3,2:T(8,128)(2,1)S(1)} %pad_maximum_fusion) | data formatting | bytes 8388608 | tf_op jit(solution)/shard_map/stack | solution.py:37
  133.2 22.5 %all-to-all-done.3 = bf16[64,2,8,2,128]{4,2,3,1,0:T(8,128)(2,1)S(1)} async-done(((bf16[64,2,8,2,128]{4,2,3,1,0:T(8,128)(2,1)}), bf16[64,2,8,2,128]{4,2,3,1,0:T(8,128)(2,1)S(1)}, u32[]{:S(2)}, u32[]{:S(2)}) %all-to-all-start.3) | async-done | bytes 524320 | tf_op jit(solution)/shard_map/all_to_all | solution.py:60
  155.7 4.8 %all-to-all-start.2 = ((bf16[64,128,2,128]{1,3,2,0:T(8,128)(2,1)}), bf16[64,128,2,128]{1,3,2,0:T(8,128)(2,1)}, u32[]{:S(2)}, u32[]{:S(2)}) async-start(bf16[64,128,2,128]{1,3,2,0:T(8,128)(2,1)} %copy.24), calls=%async_computation.2 | async-start | bytes 8388608 | tf_op jit(solution)/shard_map/all_to_all | solution.py:69
  161.7 0.8 fusion.3
  162.4 0.8 fusion.2
  163.6 4.7 %copy.29 = bf16[64,128,2,128]{1,3,2,0:T(8,128)(2,1)} copy(bf16[64,128,2,128]{1,0,3,2:T(8,128)(2,1)S(1)} %pad_maximum_fusion.1) | data formatting | bytes 8388608 | tf_op jit(solution)/shard_map/stack | solution.py:37
  168.3 43.0 %all-to-all-done.2 = bf16[64,128,2,128]{1,3,2,0:T(8,128)(2,1)} async-done(((bf16[64,128,2,128]{1,3,2,0:T(8,128)(2,1)}), bf16[64,128,2,128]{1,3,2,0:T(8,128)(2,1)}, u32[]{:S(2)}, u32[]{:S(2)}) %all-to-all-start.2) | async-done | bytes 4194336 | tf_op jit(solution)/shard_map/all_to_all | solution.py:69
  211.4 4.6 %all-to-all-start.4 = ((bf16[64,128,2,128]{1,3,2,0:T(8,128)(2,1)}), bf16[64,128,2,128]{1,3,2,0:T(8,128)(2,1)}, u32[]{:S(2)}, u32[]{:S(2)}) async-start(bf16[64,128,2,128]{1,3,2,0:T(8,128)(2,1)} %copy.29), calls=%async_computation.4 | async-start | bytes 8388608 | tf_op jit(solution)/shard_map/all_to_all | solution.py:69
  215.9 4.6 %multiply_convert_fusion.5 = (bf16[1,1024,256]{2,1,0:T(8,128)(2,1)S(1)}, bf16[1,1024,256]{2,1,0:T(8,128)(2,1)S(1)}) fusion(s32[256]{0:T(256)S(1)} %iota_add_fusion, f32[1024]{0:T(1024)S(1)} %get-tuple-element.16, f32[1024]{0:T(1024)S(1)} %get-tuple-element.17), kind=kLoop, calls=%fused_computation.27 | loop fusion | flops 4718592 | bytes 1057792 | tf_op jit(solution)/shard_map/convert
  220.5 6.8 %copy.25 = bf16[8,8,128,2,128]{4,0,2,3,1:T(8,128)(2,1)} copy(bf16[8,8,128,2,128]{2,4,3,1,0:T(8,128)(2,1)} %bitcast.9) | data formatting | bytes 8388608 | tf_op jit(solution)/shard_map/all_to_all | solution.py:69
  227.3 7.3 %all_to_all.40 = bf16[8,128,2,1024]{3,1,2,0:T(8,128)(2,1)} reshape(bf16[8,128,2,8,128]{4,3,1,2,0:T(8,128)(2,1)} %bitcast.61) | data formatting | bytes 8388608 | tf_op jit(solution)/shard_map/all_to_all | solution.py:69
  234.6 31.5 %all-to-all-done.4 = bf16[64,128,2,128]{1,3,2,0:T(8,128)(2,1)} async-done(((bf16[64,128,2,128]{1,3,2,0:T(8,128)(2,1)}), bf16[64,128,2,128]{1,3,2,0:T(8,128)(2,1)}, u32[]{:S(2)}, u32[]{:S(2)}) %all-to-all-start.4) | async-done | bytes 4194336 | tf_op jit(solution)/shard_map/all_to_all | solution.py:69
  266.0 6.8 %copy.30 = bf16[8,8,128,2,128]{4,0,2,3,1:T(8,128)(2,1)} copy(bf16[8,8,128,2,128]{2,4,3,1,0:T(8,128)(2,1)} %bitcast.21) | data formatting | bytes 8388608 | tf_op jit(solution)/shard_map/all_to_all | solution.py:69
  272.8 7.3 %all_to_all.45 = bf16[8,128,2,1024]{3,1,2,0:T(8,128)(2,1)} reshape(bf16[8,128,2,8,128]{4,3,1,2,0:T(8,128)(2,1)} %bitcast.62) | data formatting | bytes 8388608 | tf_op jit(solution)/shard_map/all_to_all | solution.py:69
  280.1 3.6 %convolution_bitcast_fusion.1 = f32[1,8,128,256]{3,2,1,0:T(8,128)S(1)} fusion(bf16[8,128,2,1024]{3,1,2,0:T(8,128)(2,1)} %all_to_all.40, bf16[1,1024,256]{2,1,0:T(8,128)(2,1)S(1)} %get-tuple-element.15, bf16[1,1024,256]{2,1,0:T(8,128)(2,1)S(1)} %get-tuple-element.14), kind=kOutput, calls=%fused_computation.17 | convolution fusion | flops 1074266112 | bytes 6291456 | tf_op jit(solution)/shard_map/scpf,pfl->scl/dot_general | solution.py:67
  283.7 1.3 convolution_bitcast_fusion
  285.0 1.5 pad_maximum_fusion.2
  (19 shorter events, 6.1 us)
Async XLA Ops:
  29.0 48.4 %all-to-all-start = ((bf16[64,2,8,2,128]{4,2,3,1,0:T(8,128)(2,1)}), bf16[64,2,8,2,128]{4,2,3,1,0:T(8,128)(2,1)S(1)}, u32[]{:S(2)}, u32[]{:S(2)}) async-start(bf16[64,2,8,2,128]{4,2,3,1,0:T(8,128)(2,1)} %bitcast.1), calls=%async_computation | async-start | bytes 1048576 | tf_op jit(solution)/shard_map/all_to_all | solution.py:48
  79.0 38.3 %all-to-all-start.1 = ((bf16[64,2,8,2,128]{4,2,3,1,0:T(8,128)(2,1)}), bf16[64,2,8,2,128]{4,2,3,1,0:T(8,128)(2,1)S(1)}, u32[]{:S(2)}, u32[]{:S(2)}) async-start(bf16[64,2,8,2,128]{4,2,3,1,0:T(8,128)(2,1)} %broadcast_select_fusion.1), calls=%async_computation.1 | async-start | bytes 1048576 | tf_op jit(solution)/shard_map/all_to_all | solution.py:60
  117.3 38.3 %all-to-all-start.3 = ((bf16[64,2,8,2,128]{4,2,3,1,0:T(8,128)(2,1)}), bf16[64,2,8,2,128]{4,2,3,1,0:T(8,128)(2,1)S(1)}, u32[]{:S(2)}, u32[]{:S(2)}) async-start(bf16[64,2,8,2,128]{4,2,3,1,0:T(8,128)(2,1)} %broadcast_select_fusion), calls=%async_computation.3 | async-start | bytes 1048576 | tf_op jit(solution)/shard_map/all_to_all | solution.py:60
  155.7 55.7 %all-to-all-start.2 = ((bf16[64,128,2,128]{1,3,2,0:T(8,128)(2,1)}), bf16[64,128,2,128]{1,3,2,0:T(8,128)(2,1)}, u32[]{:S(2)}, u32[]{:S(2)}) async-start(bf16[64,128,2,128]{1,3,2,0:T(8,128)(2,1)} %copy.24), calls=%async_computation.2 | async-start | bytes 8388608 | tf_op jit(solution)/shard_map/all_to_all | solution.py:69
  211.4 54.7 %all-to-all-start.4 = ((bf16[64,128,2,128]{1,3,2,0:T(8,128)(2,1)}), bf16[64,128,2,128]{1,3,2,0:T(8,128)(2,1)}, u32[]{:S(2)}, u32[]{:S(2)}) async-start(bf16[64,128,2,128]{1,3,2,0:T(8,128)(2,1)} %copy.29), calls=%async_computation.4 | async-start | bytes 8388608 | tf_op jit(solution)/shard_map/all_to_all | solution.py:69
  280.1 3.6 %copy-start = (bf16[8,128,2,1024]{3,1,2,0:T(8,128)(2,1)S(1)}, bf16[8,128,2,1024]{3,1,2,0:T(8,128)(2,1)}, u32[]{:S(2)}) copy-start(bf16[8,128,2,1024]{3,1,2,0:T(8,128)(2,1)} %all_to_all.45) | copy-start | bytes 12582916
where the time goes:
time: 288 us; the launch traced here: 286 us
  waiting for transfers between devices  160 us (56%)
  local copies, waits for them, and re-layouts  43.2 us (15%)
  starting transfers between devices  36.4 us (13%)
  blocking collectives  24.5 us (9%)
  other arithmetic  14.2 us (5%)
  matrix products  7.98 us (3%)
    all_to_all x2, waiting for transfers between devices, per_device(): lax.all_to_all(spectrum, 'freq', split_axis=0, concat_axis=3, tiled=True)  74.5 us
    all_to_all x2, waiting for transfers between devices, per_device(): lax.all_to_all(slots, 'grp', split_axis=0, concat_axis=0, tiled=True)  53.6 us
    all_to_all x1, waiting for transfers between devices, per_device(): lax.all_to_all(whitened_spectra.reshape(group_count, per_slot, win_count,...  31.9 us
    all_to_all x4, local copies, waits for them, and re-layouts, per_device(): lax.all_to_all(spectrum, 'freq', split_axis=0, concat_axis=3, tiled=True)  28.1 us
    psum x1, blocking collectives, per_device(): lax.psum(jnp.sum(jnp.square(spectra.astype(jnp.float32)), axis=(1, 2, 3))...  24.5 us
    all_to_all x1, starting transfers between devices, per_device(): lax.all_to_all(whitened_spectra.reshape(group_count, per_slot, win_count,...  15.8 us
    all_to_all x2, starting transfers between devices, per_device(): lax.all_to_all(slots, 'grp', split_axis=0, concat_axis=0, tiled=True)  11.2 us
    all_to_all x2, starting transfers between devices, per_device(): lax.all_to_all(spectrum, 'freq', split_axis=0, concat_axis=3, tiled=True)  9.37 us
  transfers between devices with their start and end apart: 5, of which 5 were waited for; matrix products, arithmetic and copies ran while one was open for 11% of the time, Pallas kernels for 0%

commit v1 on v0

v1 whole, which is shorter than its diff:
```python
import functools
import math

import jax
import jax.numpy as jnp
import numpy as np
from jax import lax
from jax.experimental import pallas as pl
from jax.experimental.pallas import tpu as pltpu
from jax.sharding import PartitionSpec as P

LAGS = 256
VIRTUAL_SOURCES = 64
ROUNDS = 2
MESH = pl.DeviceIdType.MESH
CHUNKS = 4


def lag_table(freq_total):
    bins = np.arange(freq_total)
    shifts = np.arange(LAGS) - LAGS // 2
    theta = (bins[:, None] * shifts[None, :] % (2 * freq_total)) * (math.pi / freq_total)
    weights = np.where(bins == 0, 1.0, 2.0) / (2.0 * freq_total)
    return np.stack([weights[:, None] * np.cos(theta), -weights[:, None] * np.sin(theta)])


def spread_table(sources, k):
    table = np.zeros((sources, k, sources, 2, 16, k), np.float32)
    for s in range(sources):
        for w in range(k // 2):
            table[s, 2 * w, s, 0, :, 2 * w] = 1.0
            table[s, 2 * w + 1, s, 0, :, 2 * w + 1] = 1.0
            table[s, 2 * w + 1, s, 1, :, 2 * w] = 1.0
            table[s, 2 * w, s, 1, :, 2 * w + 1] = -1.0
    return table.reshape(sources * k, sources * 2 * 16 * k)


def exchange_kernel(
    depth, ring, denominator,
    pair, e_in, x, s2, blk, s2o,
    e_all, xn, s2n, mid, send,
    e_ss, e_rs, s_ss, s_rs, z_ss, z_rs, l_ss, l_rs, c_ss, c_rs, p_ss, p_rs, a_ss, a_rs,
):
    freqs = 2 * ring
    rows = x.shape[0] // depth
    g = lax.axis_index("grp")
    q = lax.axis_index("freq")
    z = lax.div(g, 4)
    quad = lax.rem(g, 4)
    lo = lax.div(quad, 2)
    core = lax.rem(quad, 2)
    y = lax.div(q, 2)
    hi = lax.rem(q, 2)
    up = lax.rem(y + 1, ring)
    down = lax.rem(y + ring - 1, ring)
    across = lax.rem(y + 2, ring)
    lo_dev = (z * 4 + (1 - lo) * 2 + core, q)
    core_dev = (z * 4 + lo * 2 + (1 - core), q)
    mate_dev = (g, y * 2 + 1 - hi)
    up_dev = (g, up * 2 + hi)
    down_dev = (g, down * 2 + hi)

    def z_dev(zt):
        return (zt * 4 + quad, q)

    def copy(src, dst, ss, rs, dev):
        return pltpu.make_async_remote_copy(
            src_ref=src, dst_ref=dst, send_sem=ss, recv_sem=rs, device_id=dev, device_id_type=MESH
        )

    def arrived(ref, sem):
        pltpu.make_async_copy(ref, ref, sem).wait()

    barrier = pltpu.get_barrier_semaphore()
    for d in range(1, depth):
        pl.semaphore_signal(barrier, inc=1, device_id=z_dev(lax.rem(z + d, depth)), device_id_type=MESH)
    for d in range(1, freqs):
        pl.semaphore_signal(barrier, inc=1, device_id=(g, lax.rem(q + d, freqs)), device_id_type=MESH)
    for dev in (lo_dev, core_dev):
        pl.semaphore_signal(barrier, inc=1, device_id=dev, device_id_type=MESH)
    pl.semaphore_wait(barrier, depth - 1 + freqs - 1 + 2)

    for d in range(1, freqs):
        copy(e_in, e_all.at[q], e_ss.at[d], e_rs.at[q], (g, lax.rem(q + d, freqs))).start()
    e_all[q] = e_in[...]
    for d in range(1, freqs):
        src = lax.rem(q + d, freqs)
        arrived(e_all.at[src], e_rs.at[src])
    total = e_all[0]
    for i in range(1, freqs):
        total = total + e_all[i]
    scale = lax.rsqrt(total / denominator + 1e-06)
    xn[...] = (x[...].astype(jnp.float32) * scale[0:1, :][None]).astype(jnp.bfloat16)

    def spread(d, carry):
        zt = lax.rem(z + d, depth)
        copy(xn.at[pl.ds(zt * rows, rows)], mid.at[g], z_ss.at[zt], z_rs.at[z], z_dev(zt)).start()
        return carry

    lax.fori_loop(1, depth, spread, 0)
    mid[g] = xn[pl.ds(z * rows, rows)]

    for i in range(freqs):
        s2n[i] = (s2[i].astype(jnp.float32) * scale[8 + i : 9 + i, :]).astype(jnp.bfloat16)
    for d in range(1, freqs):
        to = lax.rem(q + d, freqs)
        copy(s2n.at[to], s2o.at[q], s_ss.at[d], s_rs.at[q], (g, to)).start()
    own_s2 = pltpu.make_async_copy(s2n.at[q], s2o.at[q], s_ss.at[0])
    own_s2.start()

    def pass_on(d, carry):
        zs = lax.rem(z + depth - d, depth)
        slot = mid.at[zs * 4 + quad]

        @pl.when(d > 0)
        def _():
            arrived(slot, z_rs.at[zs])

        copy(slot, slot, l_ss.at[zs], l_rs.at[zs], lo_dev).start()
        copy(slot, slot, c_ss.at[0, zs], c_rs.at[0, zs], core_dev).start()
        return carry

    lax.fori_loop(0, depth, pass_on, 0)

    def pass_twice(d, carry):
        zs = lax.rem(z + depth - d, depth)
        slot = mid.at[zs * 4 + (1 - lo) * 2 + core]
        arrived(slot, l_rs.at[zs])
        copy(slot, slot, c_ss.at[1, zs], c_rs.at[1, zs], core_dev).start()
        return carry

    lax.fori_loop(0, depth, pass_twice, 0)

    def gathered(d, carry):
        zs = lax.rem(z + depth - d, depth)
        arrived(mid.at[zs * 4 + lo * 2 + 1 - core], c_rs.at[0, zs])
        arrived(mid.at[zs * 4 + (1 - lo) * 2 + 1 - core], c_rs.at[1, zs])
        return carry

    lax.fori_loop(0, depth, gathered, 0)

    def select(r):
        here = pl.ds(z * rows, rows)

        def step(d, carry):
            zt = lax.rem(z + d, depth)
            send[r, zt] = mid[pair[r, zt * 4 + quad]]
            copy(send.at[r, zt], blk.at[r, q, here], p_ss.at[r, zt], p_rs.at[r, z], z_dev(zt)).start()
            return carry

        lax.fori_loop(1, depth, step, 0)
        send[r, z] = mid[pair[r, z * 4 + quad]]
        pltpu.make_async_copy(send.at[r, z], blk.at[r, q, here], p_rs.at[r, z]).start()

    per_chunk = depth // CHUNKS
    span = per_chunk * rows
    half = span // 2

    def part(r, fb, j):
        return blk.at[r, fb, pl.ds(j * span, span)]

    def halves(r, fb, j, h):
        return blk.at[r, fb, pl.ds(j * span + h * half, half)]

    def first(r, j):
        for i in range(per_chunk):
            zm = j * per_chunk + i
            arrived(blk.at[r, q, pl.ds(zm * rows, rows)], p_rs.at[r, zm])
        own = part(r, q, j)
        copy(own, own, a_ss.at[r, j, 0], a_rs.at[r, j, 0], mate_dev).start()
        copy(own, own, a_ss.at[r, j, 1], a_rs.at[r, j, 1], up_dev).start()
        copy(own, own, a_ss.at[r, j, 3], a_rs.at[r, j, 3], down_dev).start()

    def second(r, j):
        mate = part(r, y * 2 + 1 - hi, j)
        arrived(mate, a_rs.at[r, j, 0])
        copy(mate, mate, a_ss.at[r, j, 2], a_rs.at[r, j, 2], up_dev).start()
        copy(mate, mate, a_ss.at[r, j, 4], a_rs.at[r, j, 4], down_dev).start()

    def third(r, j):
        for i in range(2):
            side = hi if i == 0 else 1 - hi
            arrived(part(r, down * 2 + side, j), a_rs.at[r, j, 1 + i])
            a = halves(r, down * 2 + side, j, 0)
            copy(a, a, a_ss.at[r, j, 5 + i], a_rs.at[r, j, 5 + i], up_dev).start()
            arrived(part(r, up * 2 + side, j), a_rs.at[r, j, 3 + i])
            b = halves(r, up * 2 + side, j, 1)
            copy(b, b, a_ss.at[r, j, 7 + i], a_rs.at[r, j, 7 + i], down_dev).start()

    def fourth(r, j):
        for i in range(2):
            side = hi if i == 0 else 1 - hi
            arrived(halves(r, across * 2 + side, j, 0), a_rs.at[r, j, 5 + i])
            arrived(halves(r, across * 2 + side, j, 1), a_rs.at[r, j, 7 + i])

    select(0)
    first(0, 0)
    first(0, 1)
    select(1)
    first(0, 2)
    first(0, 3)
    for j in range(CHUNKS):
        second(0, j)
    third(0, 0)
    third(0, 1)
    first(1, 0)
    third(0, 2)
    first(1, 1)
    third(0, 3)
    first(1, 2)
    first(1, 3)
    for j in range(CHUNKS):
        second(1, j)
    for j in range(CHUNKS):
        third(1, j)
    for r in range(ROUNDS):
        for j in range(CHUNKS):
            fourth(r, j)

    own_s2.wait()
    for d in range(1, freqs):
        to = lax.rem(q + d, freqs)
        arrived(s2o.at[to], s_rs.at[to])
        arrived(s2n.at[to], s_ss.at[d])
        arrived(e_in, e_ss.at[d])

    def sent(d, carry):
        zt = lax.rem(z + d, depth)

        @pl.when(d > 0)
        def _():
            arrived(mid.at[0], z_ss.at[zt])
            arrived(mid.at[0], p_ss.at[0, zt])
            arrived(mid.at[0], p_ss.at[1, zt])

        arrived(mid.at[0], l_ss.at[zt])
        arrived(mid.at[0], c_ss.at[0, zt])
        arrived(mid.at[0], c_ss.at[1, zt])
        return carry

    lax.fori_loop(0, depth, sent, 0)
    for r in range(ROUNDS):
        for j in range(CHUNKS):
            for i in range(5):
                arrived(part(r, 0, j), a_ss.at[r, j, i])
            for i in range(5, 9):
                arrived(halves(r, 0, j, 0), a_ss.at[r, j, i])


def exchange(mesh_shape, denominator, pairing, e_in, x, s2):
    freqs = mesh_shape["freq"]
    groups = mesh_shape["grp"]
    depth, ring = groups // 4, freqs // 2
    bins, k, channels = x.shape
    rows = bins // depth
    dma = pltpu.SemaphoreType.DMA
    vmem = pl.BlockSpec(memory_space=pltpu.VMEM)
    return pl.pallas_call(
        functools.partial(exchange_kernel, depth, ring, denominator),
        out_shape=(
            jax.ShapeDtypeStruct((ROUNDS, freqs, bins, k, channels), jnp.bfloat16),
            jax.ShapeDtypeStruct(s2.shape, jnp.bfloat16),
        ),
        in_specs=[pl.BlockSpec(memory_space=pltpu.SMEM), vmem, vmem, vmem],
        out_specs=(pl.BlockSpec(memory_space=pl.ANY), pl.BlockSpec(memory_space=pl.ANY)),
        scratch_shapes=[
            pltpu.VMEM((freqs,) + e_in.shape, jnp.float32),
            pltpu.VMEM(x.shape, jnp.bfloat16),
            pltpu.VMEM(s2.shape, jnp.bfloat16),
            pltpu.VMEM((groups, rows, k, channels), jnp.bfloat16),
            pltpu.VMEM((ROUNDS, depth, rows, k, channels), jnp.bfloat16),
            dma((freqs,)), dma((freqs,)),
            dma((freqs,)), dma((freqs,)),
            dma((depth,)), dma((depth,)),
            dma((depth,)), dma((depth,)),
            dma((2, depth)), dma((2, depth)),
            dma((ROUNDS, depth)), dma((ROUNDS, depth)),
            dma((ROUNDS, CHUNKS, 9)), dma((ROUNDS, CHUNKS, 9)),
        ],
        compiler_params=pltpu.CompilerParams(
            collective_id=0, has_side_effects=True, vmem_limit_bytes=32 * 2**20
        ),
        name="exchange",
    )(pairing, e_in, x, s2)


def correlate_kernel(steps, windows, blk, s2, table, picks, out, w, spec, acc):
    step = pl.program_id(0)
    bins = s2.shape[1]
    tiles = bins // 16
    sources = w.shape[1] // 2
    wide = w.shape[3]
    row = lax.broadcasted_iota(jnp.int32, (16, wide), 0)
    col = lax.broadcasted_iota(jnp.int32, (16, wide), 1)
    mask = lax.div(col, wide // 16) == row
    for n in range(2 * sources):
        v = jnp.dot(s2[0], picks[:, n * wide : (n + 1) * wide], preferred_element_type=jnp.float32)
        v = jnp.where(mask[None], v.reshape(tiles, 16, wide), 0.0)
        w[:, n] = v.astype(jnp.bfloat16)
    for t in range(tiles):
        right = jnp.concatenate(
            [blk[r, 0, t * 16 : (t + 1) * 16].reshape(wide, -1) for r in range(ROUNDS)], axis=1
        )
        x = jnp.dot(w[t].reshape(-1, wide), right, preferred_element_type=jnp.float32)
        x = (x / windows).astype(jnp.bfloat16)
        for s in range(sources):
            for part in range(2):
                n = s * 2 + part
                spec[s, part * bins + t * 16 : part * bins + (t + 1) * 16, :] = x[n * 16 : (n + 1) * 16]

    @pl.when(step == 0)
    def _():
        for s in range(sources):
            acc[s] = jnp.dot(table[0], spec[s], preferred_element_type=jnp.float32)

    @pl.when(step > 0)
    def _():
        for s in range(sources):
            acc[s] += jnp.dot(table[0], spec[s], preferred_element_type=jnp.float32)

    @pl.when(step == steps - 1)
    def _():
        channels = out.shape[2]
        for s in range(sources):
            for r in range(ROUNDS):
                out[r, s] = acc[s, :, r * channels : (r + 1) * channels].T


def correlate(windows, sources, blk, s2, table, picks):
    rounds, freqs, bins, k, channels = blk.shape
    wide = 16 * k
    return pl.pallas_call(
        functools.partial(correlate_kernel, freqs, windows),
        out_shape=jax.ShapeDtypeStruct((rounds, sources, channels, LAGS), jnp.float32),
        grid=(freqs,),
        in_specs=[
            pl.BlockSpec((rounds, 1, bins, k, channels), lambda i: (0, i, 0, 0, 0)),
            pl.BlockSpec((1,) + s2.shape[1:], lambda i: (i, 0, 0)),
            pl.BlockSpec((1,) + table.shape[1:], lambda i: (i, 0, 0)),
            pl.BlockSpec(picks.shape, lambda i: (0, 0)),
        ],
        out_specs=pl.BlockSpec((rounds, sources, channels, LAGS), lambda i: (0, 0, 0, 0)),
        scratch_shapes=[
            pltpu.VMEM((bins // 16, 2 * sources, 16, wide), jnp.bfloat16),
            pltpu.VMEM((sources, 2 * bins, rounds * channels), jnp.bfloat16),
            pltpu.VMEM((sources, LAGS, rounds * channels), jnp.float32),
        ],
        compiler_params=pltpu.CompilerParams(vmem_limit_bytes=40 * 2**20),
        name="correlate",
    )(blk, s2, table, picks)


def per_device(mesh_shape, spectra, pairing):
    channels, windows, parts, bins = spectra.shape
    freqs = mesh_shape["freq"]
    k = windows * parts
    own = VIRTUAL_SOURCES // freqs
    flat = spectra.reshape(channels, k, bins)
    energy = jnp.sum(jnp.square(flat.astype(jnp.float32)), axis=(1, 2))
    step = channels // VIRTUAL_SOURCES
    per_lane = jnp.repeat(energy[::step].reshape(freqs, own), k, axis=1)
    e_in = jnp.concatenate([jnp.broadcast_to(energy[None], (8, channels)), per_lane])
    x = flat.transpose(2, 1, 0)
    s2 = flat[::step].reshape(freqs, own * k, bins).transpose(0, 2, 1)
    table = lag_table(freqs * bins).reshape(2, freqs, bins, LAGS).transpose(1, 3, 0, 2)
    table = jnp.asarray(table.reshape(freqs, LAGS, 2 * bins), jnp.bfloat16)
    picks = jnp.asarray(spread_table(own, k), jnp.bfloat16)
    blk, s2o = exchange(mesh_shape, k * bins * freqs, pairing, e_in, x, s2)
    return correlate(windows, own, blk, s2o, table, picks)


def solution(mesh):
    placed = (P("grp", None, None, "freq"), P())
    return jax.shard_map(
        functools.partial(per_device, dict(mesh.shape)),
        mesh=mesh,
        in_specs=placed,
        out_specs=P(None, ("grp", "freq"), None, None),
        check_vma=False,
    )
```

time: 288 us -> 186 us (0.65)
  the two profiles are of different devices: /device:TPU:32 before, /device:TPU:168 now
where the time goes in v1:
time: 186 us
  Pallas kernels  166 us (89%)
  local copies, waits for them, and re-layouts  17.6 us (9%)
  other arithmetic  2.08 us (1%)
    pallas_call x1, Pallas kernels, exchange(): pl.pallas_call(functools.partial(exchange_kernel, depth, ring, denominato...  154 us
    pallas_call x1, Pallas kernels, correlate(): pl.pallas_call(functools.partial(correlate_kernel, freqs, windows), out_s...  12.2 us
    slice x2, local copies, waits for them, and re-layouts, per_device(): s2 = flat[::step].reshape(freqs, own * k, bins).transpose(0, 2, 1)  11.4 us
    unnamed x7, local copies, waits for them, and re-layouts  5.54 us

profile of v1, /device:TPU:168, one launch (start us, length us, event | category | flops | bytes accessed | tf_op | source)
XLA Modules:
  0.0 185.9 jit_solution(10966132348114646190)
XLA Ops:
  0.0 2.1 %multiply_reduce_fusion = f32[128]{0:T(128)S(1)} fusion(bf16[128,8,2,128]{3,2,1,0:T(2,128)(2,1)} %param.4), kind=kLoop, calls=%fused_computation | loop fusion | flops 786304 | bytes 524800 | tf_op jit(solution)/shard_map/reduce_sum | solution.py:359
  2.1 0.2 slice.6
  2.2 0.1 reshape.13
  2.3 0.1 broadcast_in_dim.10
  2.4 0.1 reshape.14
  2.5 2.4 %copy.6 = bf16[128,8,2,128]{0,2,1,3:T(2,128)(2,1)S(1)} copy(bf16[128,8,2,128]{3,2,1,0:T(2,128)(2,1)} %param.4) | data formatting | bytes 1048576 | tf_op args[0]
  4.9 10.9 %slice.7 = bf16[64,16,128]{0,1,2:T(8,128)(2,1)S(1)} slice(bf16[128,16,128]{0,1,2:T(8,128)(2,1)S(1)} %bitcast.5), slice={[0:128:2], [0:16:1], [0:128:1]} | slice | bytes 524288 | tf_op jit(solution)/shard_map/slice | solution.py:364
  15.8 0.6 copy.7
  16.4 0.2 copy.8
  16.6 0.0 copy-start.2
  16.6 0.7 copy-done.2
  17.2 154.0 %exchange.1 = (bf16[2,8,128,16,128]{4,3,2,1,0:T(8,128)(2,1)S(1)}, bf16[8,128,128]{2,1,0:T(8,128)(2,1)S(1)}) custom-call(s32[2,64]{1,0:T(2,128)S(1)} %copy-done.2, f32[16,128]{1,0:T(8,128)S(1)} %pad_maximum_fusion.e_in, bf16[128,16,128]{2,1,0:T(8,128)(2,1)S(1)} %bitcast.6, bf16[8,128,128]{2,1,0:T(8,128)(2,1)S(1)} %bitcast.7), custom_call_target="tpu_custom_call" | custom-call | tf_op jit(solution)/shard_map/exchange/pallas_call | solution.py:258
  171.2 0.0 copy-start
  171.2 1.2 copy-done
  172.5 0.0 copy-start.1
  172.5 1.2 copy-done.1
  173.7 12.2 %correlate.1 = f32[2,8,128,256]{3,2,1,0:T(8,128)} custom-call(bf16[2,8,128,16,128]{4,3,2,1,0:T(8,128)(2,1)S(1)} %get-tuple-element.7.blk, bf16[8,128,128]{2,1,0:T(8,128)(2,1)S(1)} %get-tuple-element.8.s2, bf16[8,256,256]{2,1,0:T(8,128)(2,1)S(1)} %copy-done.1, bf16[128,4096]{1,0:T(8,128)(2,1)S(1)} %copy-done), custom_call_target="tpu_custom_call" | custom-call | tf_op jit(solution)/shard_map/correlate/pallas_call | solution.py:332
  (2 shorter events, 0.0 us)
Async XLA Ops:
  16.6 0.7 copy-start.2
  171.2 1.2 copy-start
  172.5 1.2 copy-start.1

commit v2 on v0

v2 whole, which is shorter than its diff:
```python
import functools
import math

import jax
import jax.numpy as jnp
import numpy as np
from jax import lax
from jax.experimental import pallas as pl
from jax.experimental.pallas import tpu as pltpu
from jax.sharding import PartitionSpec as P

LAGS = 256
VIRTUAL_SOURCES = 64
ROUNDS = 2
MESH = pl.DeviceIdType.MESH
PARTS = 4
BATCH = 4
Y_FIRST = ((0, 1), (1, 1), (2, 1))


def lag_table(freq_total):
    bins = np.arange(freq_total)
    shifts = np.arange(LAGS) - LAGS // 2
    theta = (bins[:, None] * shifts[None, :] % (2 * freq_total)) * (math.pi / freq_total)
    weights = np.where(bins == 0, 1.0, 2.0) / (2.0 * freq_total)
    return np.stack([weights[:, None] * np.cos(theta), -weights[:, None] * np.sin(theta)])


def spread_table(sources, k):
    table = np.zeros((sources, k, sources, 2, 16, k), np.float32)
    for s in range(sources):
        for w in range(k // 2):
            table[s, 2 * w, s, 0, :, 2 * w] = 1.0
            table[s, 2 * w + 1, s, 0, :, 2 * w + 1] = 1.0
            table[s, 2 * w + 1, s, 1, :, 2 * w] = 1.0
            table[s, 2 * w, s, 1, :, 2 * w + 1] = -1.0
    return table.reshape(sources * k, sources * 2 * 16 * k)


def kernel(
    depth, ring, windows,
    pair, x, s2, table, picks, out,
    e_own, e_all, xn, s2n, s2o, send, blk, w, spec, acc, *rest,
):
    mids = rest[:PARTS]
    (e_ss, e_rs, s_ss, s_rs, z_ss, z_rs, l_ss, l_rs, c_ss, c_rs, p_ss, p_rs, a_ss, a_rs) = rest[PARTS:]
    freqs = 2 * ring
    bins, k, channels = x.shape
    width = bins // PARTS
    rows = width // depth
    sources = out.shape[1]
    wide = 16 * k
    tiles = width // 16
    g = lax.axis_index("grp")
    q = lax.axis_index("freq")
    z = lax.div(g, 4)
    quad = lax.rem(g, 4)
    lo = lax.div(quad, 2)
    core = lax.rem(quad, 2)
    y = lax.div(q, 2)
    hi = lax.rem(q, 2)
    up = lax.rem(y + 1, ring)
    down = lax.rem(y + ring - 1, ring)
    across = lax.rem(y + 2, ring)
    lo_quad = (1 - lo) * 2 + core
    core_quad = lo * 2 + 1 - core
    far_quad = (1 - lo) * 2 + 1 - core
    lo_dev = (z * 4 + lo_quad, q)
    core_dev = (z * 4 + core_quad, q)
    mate = y * 2 + 1 - hi
    mate_dev = (g, mate)
    up_dev = (g, up * 2 + hi)
    down_dev = (g, down * 2 + hi)

    def z_dev(zt):
        return (zt * 4 + quad, q)

    def copy(src, dst, ss, rs, dev):
        pltpu.make_async_remote_copy(
            src_ref=src, dst_ref=dst, send_sem=ss, recv_sem=rs, device_id=dev, device_id_type=MESH
        ).start()

    def arrived(ref, sem):
        pltpu.make_async_copy(ref, ref, sem).wait()

    barrier = pltpu.get_barrier_semaphore()
    for d in range(1, depth):
        pl.semaphore_signal(barrier, inc=1, device_id=z_dev(lax.rem(z + d, depth)), device_id_type=MESH)
    for d in range(1, freqs):
        pl.semaphore_signal(barrier, inc=1, device_id=(g, lax.rem(q + d, freqs)), device_id_type=MESH)
    for dev in (lo_dev, core_dev):
        pl.semaphore_signal(barrier, inc=1, device_id=dev, device_id_type=MESH)

    def square_sum(i, total):
        v = x[pl.ds(i * 8, 8)].astype(jnp.float32)
        return total + jnp.sum(v * v, axis=0)

    total = lax.fori_loop(0, bins // 8, square_sum, jnp.zeros((k, channels), jnp.float32))
    e_own[0:8] = jnp.broadcast_to(jnp.sum(total, axis=0, keepdims=True), (8, channels))
    for i in range(freqs):
        v = s2[i].astype(jnp.float32)
        e_own[8 + i : 9 + i] = jnp.sum(v * v, axis=0, keepdims=True)
    lanes = e_own.shape[1]
    same = lax.div(lax.broadcasted_iota(jnp.int32, (lanes, lanes), 0), k) == lax.div(
        lax.broadcasted_iota(jnp.int32, (lanes, lanes), 1), k
    )
    e_own[8:] = jnp.dot(
        e_own[8:], same.astype(jnp.float32), precision=lax.Precision.HIGHEST, preferred_element_type=jnp.float32
    )

    pl.semaphore_wait(barrier, depth - 1 + freqs - 1 + 2)
    for d in range(1, freqs):
        copy(e_own, e_all.at[q], e_ss.at[d], e_rs.at[q], (g, lax.rem(q + d, freqs)))
    e_all[q] = e_own[...]
    for d in range(1, freqs):
        src = lax.rem(q + d, freqs)
        arrived(e_all.at[src], e_rs.at[src])
    total = e_all[0]
    for i in range(1, freqs):
        total = total + e_all[i]
    scale = lax.rsqrt(total / (k * bins * freqs) + 1e-06)

    def spread(a):
        part = pl.ds(a * width, width)
        xn[part] = (x[part].astype(jnp.float32) * scale[0:1, :][None]).astype(jnp.bfloat16)
        slot = pl.ds(quad * depth + z, 1)

        def step(d, carry):
            zt = lax.rem(z + d, depth)
            copy(
                xn.at[pl.ds(a * width + zt * rows, rows)], mids[a].at[quad * depth + z],
                z_ss.at[a, zt], z_rs.at[a, z], z_dev(zt),
            )
            return carry

        lax.fori_loop(1, depth, step, 0)
        mids[a][slot] = xn[pl.ds(a * width + z * rows, rows)][None]

    for a in range(PARTS):
        spread(a)
    for i in range(freqs):
        s2n[i] = (s2[i].astype(jnp.float32) * scale[8 + i : 9 + i, :]).astype(jnp.bfloat16)
    for d in range(1, freqs):
        to = lax.rem(q + d, freqs)
        copy(s2n.at[to], s2o.at[q], s_ss.at[d], s_rs.at[q], (g, to))
    s2o[q] = s2n[q]

    batches = depth // BATCH

    def run(a, quarter, b):
        return mids[a].at[pl.ds(quarter * depth + b * BATCH, BATCH)]

    def pass_on(a):
        def step(i, carry):
            b = lax.rem(lax.div(z, BATCH) + i, batches)

            def one(j, carry):
                zs = b * BATCH + j

                @pl.when(zs != z)
                def _():
                    arrived(mids[a].at[quad * depth + zs], z_rs.at[a, zs])

                return carry

            lax.fori_loop(0, BATCH, one, 0)
            part = run(a, quad, b)
            copy(part, part, l_ss.at[a, b], l_rs.at[a, b], lo_dev)
            copy(part, part, c_ss.at[a, 0, b], c_rs.at[a, 0, b], core_dev)
            return carry

        lax.fori_loop(0, batches, step, 0)

    def pass_twice(a):
        def step(i, carry):
            b = lax.rem(lax.div(z, BATCH) + i, batches)
            part = run(a, lo_quad, b)
            arrived(part, l_rs.at[a, b])
            copy(part, part, c_ss.at[a, 1, b], c_rs.at[a, 1, b], core_dev)
            return carry

        lax.fori_loop(0, batches, step, 0)

    def passed(a):
        for b in range(batches):
            arrived(run(a, core_quad, b), c_rs.at[a, 0, b])
            arrived(run(a, far_quad, b), c_rs.at[a, 1, b])

    def select(a, r):
        here = pl.ds(z * rows, rows)

        def wanted(zt):
            p = pair[r, zt * 4 + quad]
            return mids[a][lax.rem(p, 4) * depth + lax.div(p, 4)]

        def step(d, carry):
            zt = lax.rem(z + d, depth)
            send[a, r, zt] = wanted(zt)
            copy(send.at[a, r, zt], blk.at[a, q, r, here], p_ss.at[a, r, zt], p_rs.at[a, r, z], z_dev(zt))
            return carry

        lax.fori_loop(1, depth, step, 0)
        blk[a, q, r, here] = wanted(z)

    half = width // 2

    def block(a, r, fb):
        return blk.at[a, fb, r]

    def halves(a, r, fb, h):
        return blk.at[a, fb, r, pl.ds(h * half, half)]

    def ship(ref, a, r, i, dev):
        copy(ref, ref, a_ss.at[a, r, i], a_rs.at[a, r, i], dev)

    def first(a, r):
        def one(d, carry):
            zm = lax.rem(z + d, depth)
            arrived(blk.at[a, q, r, pl.ds(zm * rows, rows)], p_rs.at[a, r, zm])
            return carry

        lax.fori_loop(1, depth, one, 0)
        own = block(a, r, q)
        ship(own, a, r, 1, up_dev)
        ship(own, a, r, 3, down_dev)
        ship(own, a, r, 0, mate_dev)

    def second(a, r):
        if (a, r) in Y_FIRST:
            return
        other = block(a, r, mate)
        arrived(other, a_rs.at[a, r, 0])
        ship(other, a, r, 2, up_dev)
        ship(other, a, r, 4, down_dev)

    def third(a, r):
        for i in range(1 if (a, r) in Y_FIRST else 2):
            side = hi if i == 0 else 1 - hi
            low, high = down * 2 + side, up * 2 + side
            arrived(block(a, r, low), a_rs.at[a, r, 1 + i])
            ship(halves(a, r, low, 0), a, r, 5 + i, up_dev)
            arrived(block(a, r, high), a_rs.at[a, r, 3 + i])
            ship(halves(a, r, high, 1), a, r, 7 + i, down_dev)
            if (a, r) in Y_FIRST:
                ship(block(a, r, low), a, r, 2, mate_dev)
                ship(block(a, r, high), a, r, 4, mate_dev)

    def fourth(a, r):
        if (a, r) in Y_FIRST:
            arrived(halves(a, r, across * 2 + hi, 0), a_rs.at[a, r, 5])
            arrived(halves(a, r, across * 2 + hi, 1), a_rs.at[a, r, 7])
            ship(block(a, r, across * 2 + hi), a, r, 6, mate_dev)
            return
        for i in range(2):
            side = hi if i == 0 else 1 - hi
            arrived(halves(a, r, across * 2 + side, 0), a_rs.at[a, r, 5 + i])
            arrived(halves(a, r, across * 2 + side, 1), a_rs.at[a, r, 7 + i])

    def last(a, r):
        if (a, r) in Y_FIRST:
            arrived(block(a, r, mate), a_rs.at[a, r, 0])
            arrived(block(a, r, down * 2 + 1 - hi), a_rs.at[a, r, 2])
            arrived(block(a, r, up * 2 + 1 - hi), a_rs.at[a, r, 4])
            arrived(block(a, r, across * 2 + 1 - hi), a_rs.at[a, r, 6])

    def weights(a):
        row = lax.broadcasted_iota(jnp.int32, (16, wide), 0)
        col = lax.broadcasted_iota(jnp.int32, (16, wide), 1)
        mask = lax.div(col, k) == row

        def step(fb, carry):
            v = s2o[fb, a * width : (a + 1) * width, :]
            for n in range(2 * sources):
                u = jnp.dot(v, picks[:, n * wide : (n + 1) * wide], preferred_element_type=jnp.float32)
                w[a, fb, :, n] = jnp.where(mask[None], u.reshape(tiles, 16, wide), 0.0).astype(jnp.bfloat16)
            return carry

        lax.fori_loop(0, freqs, step, 0)

    def correlate(a):
        def step(fb, carry):
            for t in range(tiles):
                right = jnp.concatenate(
                    [blk[a, fb, r, t * 16 : (t + 1) * 16].reshape(wide, channels) for r in range(ROUNDS)], axis=1
                )
                v = jnp.dot(w[a, fb, t].reshape(2 * sources * 16, wide), right, preferred_element_type=jnp.float32)
                v = (v * (1.0 / windows)).astype(jnp.bfloat16)
                for s in range(sources):
                    for part in range(2):
                        n = s * 2 + part
                        at = pl.multiple_of(fb * (2 * width) + part * width + t * 16, 16)
                        spec[s, pl.ds(at, 16), :] = v[n * 16 : (n + 1) * 16]
            return carry

        lax.fori_loop(0, freqs, step, 0)
        span = 2 * width * freqs

        def lags(s, carry):
            v = jnp.dot(table[:, a * span : (a + 1) * span], spec[s], preferred_element_type=jnp.float32)
            if a > 0:
                v = v + acc[s]
            if a == PARTS - 1:
                for r in range(ROUNDS):
                    out[r, s] = v[:, r * channels : (r + 1) * channels].T
            else:
                acc[s] = v
            return carry

        lax.fori_loop(0, sources, lags, 0)

    turns = [(a, r) for a in range(PARTS) for r in range(ROUNDS)]
    pass_on(0)
    pass_twice(0)
    passed(0)
    select(*turns[0])
    for a in range(1, PARTS):
        pass_on(a)
        pass_twice(a)
        if a == 1:
            select(*turns[1])
        passed(a)
    for d in range(1, freqs):
        src = lax.rem(q + d, freqs)
        arrived(s2o.at[src], s_rs.at[src])
    ahead = 2
    for i in range(len(turns) + 3):
        if i < len(turns):
            first(*turns[i])
            if i + ahead < len(turns):
                select(*turns[i + ahead])
            second(*turns[i])
        if 0 <= i - 1 < len(turns):
            third(*turns[i - 1])
        if 0 <= i - 2 < len(turns):
            fourth(*turns[i - 2])
        if 0 <= i - 3 < len(turns):
            last(*turns[i - 3])
        if i < PARTS:
            weights(i)
        if i >= 3 and (i - 3) % ROUNDS == ROUNDS - 1:
            correlate((i - 3) // ROUNDS)

    for d in range(1, freqs):
        arrived(s2n.at[0], s_ss.at[d])
        arrived(e_own, e_ss.at[d])
    for a in range(PARTS):
        def sent(d, carry):
            zt = lax.rem(z + d, depth)
            arrived(mids[a].at[0], z_ss.at[a, zt])
            for r in range(ROUNDS):
                arrived(mids[a].at[0], p_ss.at[a, r, zt])
            return carry

        lax.fori_loop(1, depth, sent, 0)
        for b in range(batches):
            arrived(run(a, 0, b), l_ss.at[a, b])
            arrived(run(a, 0, b), c_ss.at[a, 0, b])
            arrived(run(a, 0, b), c_ss.at[a, 1, b])
        for r in range(ROUNDS):
            y_first = (a, r) in Y_FIRST
            for i in range(9):
                if y_first and i == 8:
                    continue
                whole = i < 5 or (y_first and i == 6)
                arrived(block(a, r, 0) if whole else halves(a, r, 0, 0), a_ss.at[a, r, i])


def per_device(mesh_shape, spectra, pairing):
    channels, windows, two, bins = spectra.shape
    freqs, groups = mesh_shape["freq"], mesh_shape["grp"]
    depth, ring = groups // 4, freqs // 2
    k = windows * two
    sources = VIRTUAL_SOURCES // freqs
    width = bins // PARTS
    rows = width // depth
    step = channels // VIRTUAL_SOURCES
    x = spectra.reshape(channels, k, bins).transpose(2, 1, 0)
    s2 = spectra.reshape(VIRTUAL_SOURCES, step, k, bins)[:, 0]
    s2 = lax.optimization_barrier(s2).reshape(freqs, sources * k, bins).transpose(0, 2, 1)
    table = lag_table(freqs * bins).reshape(2, freqs, PARTS, width, LAGS).transpose(4, 2, 1, 0, 3)
    table = jnp.asarray(table.reshape(LAGS, 2 * freqs * bins), jnp.bfloat16)
    picks = jnp.asarray(spread_table(sources, k), jnp.bfloat16)
    dma = pltpu.SemaphoreType.DMA
    vmem = pl.BlockSpec(memory_space=pltpu.VMEM)
    bf16, f32 = jnp.bfloat16, jnp.float32
    return pl.pallas_call(
        functools.partial(kernel, depth, ring, windows),
        out_shape=jax.ShapeDtypeStruct((ROUNDS, sources, channels, LAGS), f32),
        in_specs=[pl.BlockSpec(memory_space=pltpu.SMEM), vmem, vmem, vmem, vmem],
        out_specs=vmem,
        scratch_shapes=[
            pltpu.VMEM((8 + freqs, channels), f32),
            pltpu.VMEM((freqs, 8 + freqs, channels), f32),
            pltpu.VMEM(x.shape, bf16),
            pltpu.VMEM(s2.shape, bf16),
            pltpu.VMEM(s2.shape, bf16),
            pltpu.VMEM((PARTS, ROUNDS, depth, rows, k, channels), bf16),
            pltpu.VMEM((PARTS, freqs, ROUNDS, width, k, channels), bf16),
            pltpu.VMEM((PARTS, freqs, width // 16, 2 * sources, 16, 16 * k), bf16),
            pltpu.VMEM((sources, 2 * width * freqs, ROUNDS * channels), bf16),
            pltpu.VMEM((sources, LAGS, ROUNDS * channels), f32),
        ]
        + [pltpu.VMEM((groups, rows, k, channels), bf16)] * PARTS
        + [
            dma((freqs,)), dma((freqs,)),
            dma((freqs,)), dma((freqs,)),
            dma((PARTS, depth)), dma((PARTS, depth)),
            dma((PARTS, depth // BATCH)), dma((PARTS, depth // BATCH)),
            dma((PARTS, 2, depth // BATCH)), dma((PARTS, 2, depth // BATCH)),
            dma((PARTS, ROUNDS, depth)), dma((PARTS, ROUNDS, depth)),
            dma((PARTS, ROUNDS, 9)), dma((PARTS, ROUNDS, 9)),
        ],
        compiler_params=pltpu.CompilerParams(
            collective_id=0, has_side_effects=True, vmem_limit_bytes=48 * 2**20
        ),
        name="correlate_pairs",
    )(pairing, x, s2, table, picks)


def solution(mesh):
    placed = (P("grp", None, None, "freq"), P())
    return jax.shard_map(
        functools.partial(per_device, dict(mesh.shape)),
        mesh=mesh,
        in_specs=placed,
        out_specs=P(None, ("grp", "freq"), None, None),
        check_vma=False,
    )
```

time: 288 us -> 141 us (0.49)
  the two profiles are of different devices: /device:TPU:32 before, /device:TPU:10 now
where the time goes in v2:
time: 141 us
  Pallas kernels  136 us (96%)
  local copies, waits for them, and re-layouts  5.05 us (4%)
    pallas_call x1, Pallas kernels, per_device(): pl.pallas_call(functools.partial(kernel, depth, ring, windows), out_shape...  136 us
    unnamed x8, local copies, waits for them, and re-layouts  3.75 us

profile of v2, /device:TPU:10, one launch (start us, length us, event | category | flops | bytes accessed | tf_op | source)
XLA Modules:
  0.0 141.3 jit_solution(14653101562448315417)
XLA Ops:
  0.0 0.0 copy-start
  0.0 0.0 copy-start.1
  0.0 0.0 copy-start.2
  0.0 1.1 slice_bitcast_fusion
  1.1 0.2 copy.9
  1.3 2.4 %copy.8 = bf16[128,8,2,128]{0,2,1,3:T(2,128)(2,1)S(1)} copy(bf16[128,8,2,128]{3,2,1,0:T(2,128)(2,1)} %param.4) | data formatting | bytes 1048576 | tf_op args[0]
  3.7 0.0 copy-done
  3.8 0.0 copy-done.1
  3.8 0.0 copy-done.2
  3.8 136.2 %correlate_pairs.1 = f32[2,8,128,256]{3,2,1,0:T(8,128)S(1)} custom-call(s32[2,64]{1,0:T(2,128)S(1)} %copy-done.2, bf16[128,16,128]{2,1,0:T(8,128)(2,1)S(1)} %bitcast.8, bf16[8,128,128]{2,1,0:T(8,128)(2,1)S(1)} %bitcast.9, bf16[256,2048]{1,0:T(8,128)(2,1)S(1)} %copy-done.1, bf16[128,4096]{1,0:T(8,128)(2,1)S(1)} %copy-done), custom_call_target="tpu_custom_call" | custom-call | tf_op jit(solution)/shard_map/correlate_pairs/pallas_call | solution.py:386
  140.0 1.3 copy.11
Async XLA Ops:
  0.0 3.7 %copy-start = (bf16[128,4096]{1,0:T(8,128)(2,1)S(1)}, bf16[128,4096]{1,0:T(8,128)(2,1)}, u32[]{:S(2)}) copy-start(bf16[128,4096]{1,0:T(8,128)(2,1)} %constant.5.clone.picks) | copy-start | bytes 3145732
  0.0 3.7 %copy-start.1 = (bf16[256,2048]{1,0:T(8,128)(2,1)S(1)}, bf16[256,2048]{1,0:T(8,128)(2,1)}, u32[]{:S(2)}) copy-start(bf16[256,2048]{1,0:T(8,128)(2,1)} %constant.4.clone.table) | copy-start | bytes 3145732
  0.0 3.8 %copy-start.2 = (s32[2,64]{1,0:T(2,128)S(1)}, s32[2,64]{1,0:T(2,128)}, u32[]{:S(2)}) copy-start(s32[2,64]{1,0:T(2,128)} %pair.1) | copy-start | bytes 1540

commit v3 on v2

--- a/solution.py
+++ b/solution.py
@@ -16,6 +16,14 @@
 PARTS = 4
 BATCH = 4
 Y_FIRST = ((0, 1), (1, 1), (2, 1))
+ORDER = (
+    ("E0", "Z1", "P0", "Z2", "E1", "Q0", "E2", "R0", "X0", "P1", "Q1", "R1", "X1", "O0", "E3", "W0")
+    + ("F0", "X2", "P2", "Q2", "W1", "Z3", "F1", "S0", "X3", "R2", "F2", "X4", "S1", "T0", "P3", "Q3")
+    + ("F3", "X5", "S2", "T1", "U0", "R3", "F4", "X6", "S3", "T2", "U1", "L0", "F5", "X7", "S4", "T3")
+    + ("U2", "L1", "A0", "F6", "S5", "B0", "T4", "U3", "G0", "L2", "F7", "S6", "T5", "U4", "L3", "S7")
+    + ("A1", "T6", "B1", "U5", "G1", "L4", "T7", "U6", "L5", "A2", "B2", "G2", "A3", "U7", "L6", "L7")
+    + ("B3", "G3", "z0", "z1", "z2", "z3", "s0", "s1", "s2", "s3", "s4", "s5", "s6", "s7")
+)
 
 
 def lag_table(freq_total):
@@ -40,10 +48,10 @@
 def kernel(
     depth, ring, windows,
     pair, x, s2, table, picks, out,
-    e_own, e_all, xn, s2n, s2o, send, blk, w, spec, acc, *rest,
+    e_own, e_all, e_sum, e_grp, norm, s2o, send, blk, w, spec, acc, *rest,
 ):
     mids = rest[:PARTS]
-    (e_ss, e_rs, s_ss, s_rs, z_ss, z_rs, l_ss, l_rs, c_ss, c_rs, p_ss, p_rs, a_ss, a_rs) = rest[PARTS:]
+    (e_ss, e_rs, g_ss, g_rs, t_ss, t_rs, s_ss, s_rs, z_ss, z_rs, l_ss, l_rs, c_ss, c_rs, p_ss, p_rs, a_ss, a_rs) = rest[PARTS:]
     freqs = 2 * ring
     bins, k, channels = x.shape
     width = bins // PARTS
@@ -75,6 +83,10 @@
     def z_dev(zt):
         return (zt * 4 + quad, q)
 
+    def place(i):
+        d = lax.div(i + 1, 2)
+        return lax.rem(z + i, depth)
+
     def copy(src, dst, ss, rs, dev):
         pltpu.make_async_remote_copy(
             src_ref=src, dst_ref=dst, send_sem=ss, recv_sem=rs, device_id=dev, device_id_type=MESH
@@ -109,41 +121,70 @@
     )
 
     pl.semaphore_wait(barrier, depth - 1 + freqs - 1 + 2)
+
+    def spread(a):
+        def step(i, carry):
+            zt = place(i)
+            copy(
+                x.at[pl.ds(a * width + zt * rows, rows)], mids[a].at[quad * depth + z],
+                z_ss.at[a, zt], z_rs.at[a, z], z_dev(zt),
+            )
+            return carry
+
+        lax.fori_loop(1, depth, step, 0)
+        mids[a][pl.ds(quad * depth + z, 1)] = x[pl.ds(a * width + z * rows, rows)][None]
+
+    spread(0)
     for d in range(1, freqs):
-        copy(e_own, e_all.at[q], e_ss.at[d], e_rs.at[q], (g, lax.rem(q + d, freqs)))
+        to = lax.rem(q + d, freqs)
+        copy(e_own, e_all.at[q], e_ss.at[d], e_rs.at[q], (g, to))
     e_all[q] = e_own[...]
     for d in range(1, freqs):
-        src = lax.rem(q + d, freqs)
-        arrived(e_all.at[src], e_rs.at[src])
-    total = e_all[0]
-    for i in range(1, freqs):
-        total = total + e_all[i]
-    scale = lax.rsqrt(total / (k * bins * freqs) + 1e-06)
-
-    def spread(a):
-        part = pl.ds(a * width, width)
-        xn[part] = (x[part].astype(jnp.float32) * scale[0:1, :][None]).astype(jnp.bfloat16)
-        slot = pl.ds(quad * depth + z, 1)
-
-        def step(d, carry):
-            zt = lax.rem(z + d, depth)
-            copy(
-                xn.at[pl.ds(a * width + zt * rows, rows)], mids[a].at[quad * depth + z],
-                z_ss.at[a, zt], z_rs.at[a, z], z_dev(zt),
-            )
-            return carry
-
-        lax.fori_loop(1, depth, step, 0)
-        mids[a][slot] = xn[pl.ds(a * width + z * rows, rows)][None]
-
-    for a in range(PARTS):
-        spread(a)
-    for i in range(freqs):
-        s2n[i] = (s2[i].astype(jnp.float32) * scale[8 + i : 9 + i, :]).astype(jnp.bfloat16)
-    for d in range(1, freqs):
         to = lax.rem(q + d, freqs)
-        copy(s2n.at[to], s2o.at[q], s_ss.at[d], s_rs.at[q], (g, to))
-    s2o[q] = s2n[q]
+        copy(s2.at[to], s2o.at[q], s_ss.at[d], s_rs.at[q], (g, to))
+    s2o[q] = s2[q]
+
+    def energy_run(quarter):
+        return e_grp.at[pl.ds(quarter * depth, depth)]
+
+    def energies(step):
+        if step == 0:
+            for d in range(1, freqs):
+                src = lax.rem(q + d, freqs)
+                arrived(e_all.at[src], e_rs.at[src])
+            total = e_all[0]
+            for i in range(1, freqs):
+                total = total + e_all[i]
+            e_sum[...] = total
+            e_grp[quad * depth + z] = total[0:8]
+
+            def one(i, carry):
+                zt = place(i)
+                copy(e_sum.at[pl.ds(0, 8)], e_grp.at[quad * depth + z], g_ss.at[zt], g_rs.at[z], z_dev(zt))
+                return carry
+
+            lax.fori_loop(1, depth, one, 0)
+        if step == 1:
+            def one(d, carry):
+                zs = lax.rem(z + d, depth)
+                arrived(e_grp.at[quad * depth + zs], g_rs.at[zs])
+                return carry
+
+            lax.fori_loop(1, depth, one, 0)
+            copy(energy_run(quad), energy_run(quad), t_ss.at[0], t_rs.at[0], lo_dev)
+            copy(energy_run(quad), energy_run(quad), t_ss.at[1], t_rs.at[1], core_dev)
+        if step == 2:
+            arrived(energy_run(lo_quad), t_rs.at[0])
+            copy(energy_run(lo_quad), energy_run(lo_quad), t_ss.at[2], t_rs.at[2], core_dev)
+        if step == 3:
+            arrived(energy_run(core_quad), t_rs.at[1])
+            arrived(energy_run(far_quad), t_rs.at[2])
+            count = k * bins * freqs
+            for r in range(ROUNDS):
+                p = pair[r, g]
+                norm[r] = lax.rsqrt(e_grp[lax.rem(p, 4) * depth + lax.div(p, 4)] / count + 1e-06)
+            own = e_sum[pl.ds(8 + q, 1)]
+            norm[ROUNDS] = jnp.broadcast_to(lax.rsqrt(own / count + 1e-06), (8, channels))
 
     batches = depth // BATCH
 
@@ -193,8 +234,8 @@
             p = pair[r, zt * 4 + quad]
             return mids[a][lax.rem(p, 4) * depth + lax.div(p, 4)]
 
-        def step(d, carry):
-            zt = lax.rem(z + d, depth)
+        def step(i, carry):
+            zt = place(i)
             send[a, r, zt] = wanted(zt)
             copy(send.at[a, r, zt], blk.at[a, q, r, here], p_ss.at[a, r, zt], p_rs.at[a, r, z], z_dev(zt))
             return carry
@@ -263,27 +304,39 @@
             arrived(block(a, r, up * 2 + 1 - hi), a_rs.at[a, r, 4])
             arrived(block(a, r, across * 2 + 1 - hi), a_rs.at[a, r, 6])
 
-    def weights(a):
+    def weights(part):
         row = lax.broadcasted_iota(jnp.int32, (16, wide), 0)
         col = lax.broadcasted_iota(jnp.int32, (16, wide), 1)
         mask = lax.div(col, k) == row
-
-        def step(fb, carry):
-            v = s2o[fb, a * width : (a + 1) * width, :]
-            for n in range(2 * sources):
+        near = freqs // 2
+
+        def step(i, carry):
+            at = pl.ds(i * near, near)
+            v = s2o[at].astype(jnp.float32) * norm[ROUNDS, 0:1][None]
+            v = v.astype(jnp.bfloat16).reshape(near * bins, sources * k)
+            for n in range(part * sources, (part + 1) * sources):
                 u = jnp.dot(v, picks[:, n * wide : (n + 1) * wide], preferred_element_type=jnp.float32)
-                w[a, fb, :, n] = jnp.where(mask[None], u.reshape(tiles, 16, wide), 0.0).astype(jnp.bfloat16)
-            return carry
-
-        lax.fori_loop(0, freqs, step, 0)
-
-    def correlate(a):
-        def step(fb, carry):
+                u = jnp.where(mask[None], u.reshape(near * bins // 16, 16, wide), 0.0).astype(jnp.bfloat16)
+                w[pl.ds(i * near * bins // 16, near * bins // 16), n] = u
+            return carry
+
+        lax.fori_loop(0, freqs // near, step, 0)
+
+    def spectra(a, row):
+        def step(side, carry):
+            fb = row * 2 + side
             for t in range(tiles):
                 right = jnp.concatenate(
-                    [blk[a, fb, r, t * 16 : (t + 1) * 16].reshape(wide, channels) for r in range(ROUNDS)], axis=1
+                    [
+                        (blk[a, fb, r, t * 16 : (t + 1) * 16].astype(jnp.float32) * norm[r, 0:1][None])
+                        .astype(jnp.bfloat16)
+                        .reshape(wide, channels)
+                        for r in range(ROUNDS)
+                    ],
+                    axis=1,
                 )
-                v = jnp.dot(w[a, fb, t].reshape(2 * sources * 16, wide), right, preferred_element_type=jnp.float32)
+                left = w[fb * (bins // 16) + a * tiles + t].reshape(2 * sources * 16, wide)
+                v = jnp.dot(left, right, preferred_element_type=jnp.float32)
                 v = (v * (1.0 / windows)).astype(jnp.bfloat16)
                 for s in range(sources):
                     for part in range(2):
@@ -292,7 +345,13 @@
                         spec[s, pl.ds(at, 16), :] = v[n * 16 : (n + 1) * 16]
             return carry
 
-        lax.fori_loop(0, freqs, step, 0)
+        lax.fori_loop(0, 2, step, 0)
+
+    def near_spectra(a):
+        for row in (y, up, down):
+            spectra(a, row)
+
+    def lags_of(a):
         span = 2 * width * freqs
 
         def lags(s, carry):
@@ -309,49 +368,61 @@
         lax.fori_loop(0, sources, lags, 0)
 
     turns = [(a, r) for a in range(PARTS) for r in range(ROUNDS)]
-    pass_on(0)
-    pass_twice(0)
-    passed(0)
-    select(*turns[0])
-    for a in range(1, PARTS):
-        pass_on(a)
-        pass_twice(a)
-        if a == 1:
-            select(*turns[1])
-        passed(a)
+
+    def spread_sent(a):
+        def one(d, carry):
+            arrived(mids[a].at[0], z_ss.at[a, lax.rem(z + d, depth)])
+            return carry
+
+        lax.fori_loop(1, depth, one, 0)
+
+    def select_sent(a, r):
+        def one(d, carry):
+            arrived(mids[a].at[0], p_ss.at[a, r, lax.rem(z + d, depth)])
+            return carry
+
+        lax.fori_loop(1, depth, one, 0)
+
+    def sources_here():
+        for d in range(1, freqs):
+            src = lax.rem(q + d, freqs)
+            arrived(s2o.at[src], s_rs.at[src])
+
+    names = {
+        "z": lambda a: spread_sent(a),
+        "s": lambda t: select_sent(*turns[t]),
+        "Z": lambda a: spread(a),
+        "P": lambda a: pass_on(a),
+        "Q": lambda a: pass_twice(a),
+        "R": lambda a: passed(a),
+        "X": lambda t: select(*turns[t]),
+        "F": lambda t: first(*turns[t]),
+        "S": lambda t: second(*turns[t]),
+        "T": lambda t: third(*turns[t]),
+        "U": lambda t: fourth(*turns[t]),
+        "L": lambda t: last(*turns[t]),
+        "O": lambda a: sources_here(),
+        "W": lambda a: weights(a),
+        "A": lambda a: near_spectra(a),
+        "B": lambda a: spectra(a, across),
+        "G": lambda a: lags_of(a),
+        "E": lambda a: energies(a),
+    }
+    for name in ORDER:
+        names[name[0]](int(name[1]))
+
     for d in range(1, freqs):
-        src = lax.rem(q + d, freqs)
-        arrived(s2o.at[src], s_rs.at[src])
-    ahead = 2
-    for i in range(len(turns) + 3):
-        if i < len(turns):
-            first(*turns[i])
-            if i + ahead < len(turns):
-                select(*turns[i + ahead])
-            second(*turns[i])
-        if 0 <= i - 1 < len(turns):
-            third(*turns[i - 1])
-        if 0 <= i - 2 < len(turns):
-            fourth(*turns[i - 2])
-        if 0 <= i - 3 < len(turns):
-            last(*turns[i - 3])
-        if i < PARTS:
-            weights(i)
-        if i >= 3 and (i - 3) % ROUNDS == ROUNDS - 1:
-            correlate((i - 3) // ROUNDS)
-
-    for d in range(1, freqs):
-        arrived(s2n.at[0], s_ss.at[d])
+        arrived(s2.at[0], s_ss.at[d])
         arrived(e_own, e_ss.at[d])
+
+    def energy_sent(d, carry):
+        arrived(e_grp.at[0], g_ss.at[lax.rem(z + d, depth)])
+        return carry
+
+    lax.fori_loop(1, depth, energy_sent, 0)
+    for i in range(3):
+        arrived(energy_run(0), t_ss.at[i])
     for a in range(PARTS):
-        def sent(d, carry):
-            zt = lax.rem(z + d, depth)
-            arrived(mids[a].at[0], z_ss.at[a, zt])
-            for r in range(ROUNDS):
-                arrived(mids[a].at[0], p_ss.at[a, r, zt])
-            return carry
-
-        lax.fori_loop(1, depth, sent, 0)
         for b in range(batches):
             arrived(run(a, 0, b), l_ss.at[a, b])
             arrived(run(a, 0, b), c_ss.at[a, 0, b])
@@ -391,18 +462,21 @@
         scratch_shapes=[
             pltpu.VMEM((8 + freqs, channels), f32),
             pltpu.VMEM((freqs, 8 + freqs, channels), f32),
-            pltpu.VMEM(x.shape, bf16),
-            pltpu.VMEM(s2.shape, bf16),
+            pltpu.VMEM((8 + freqs, channels), f32),
+            pltpu.VMEM((groups, 8, channels), f32),
+            pltpu.VMEM((ROUNDS + 1, 8, channels), f32),
             pltpu.VMEM(s2.shape, bf16),
             pltpu.VMEM((PARTS, ROUNDS, depth, rows, k, channels), bf16),
             pltpu.VMEM((PARTS, freqs, ROUNDS, width, k, channels), bf16),
-            pltpu.VMEM((PARTS, freqs, width // 16, 2 * sources, 16, 16 * k), bf16),
+            pltpu.VMEM((freqs * bins // 16, 2 * sources, 16, 16 * k), bf16),
             pltpu.VMEM((sources, 2 * width * freqs, ROUNDS * channels), bf16),
             pltpu.VMEM((sources, LAGS, ROUNDS * channels), f32),
         ]
         + [pltpu.VMEM((groups, rows, k, channels), bf16)] * PARTS
         + [
             dma((freqs,)), dma((freqs,)),
+            dma((depth,)), dma((depth,)),
+            dma((3,)), dma((3,)),
             dma((freqs,)), dma((freqs,)),
             dma((PARTS, depth)), dma((PARTS, depth)),
             dma((PARTS, depth // BATCH)), dma((PARTS, depth // BATCH)),

time: 141 us -> 137 us (0.972)
  the two profiles are of different devices: /device:TPU:10 before, /device:TPU:16 now
where the time goes in v3:
time: 137 us
  Pallas kernels  131 us (96%)
  local copies, waits for them, and re-layouts  5.05 us (4%)
    pallas_call x1, Pallas kernels, per_device(): pl.pallas_call(functools.partial(kernel, depth, ring, windows), out_shape...  131 us
    unnamed x8, local copies, waits for them, and re-layouts  3.75 us

profile of v3, /device:TPU:16, one launch (start us, length us, event | category | flops | bytes accessed | tf_op | source)
XLA Modules:
  0.0 136.6 jit_solution(4401610807217222742)
XLA Ops:
  0.0 0.0 copy-start
  0.0 0.0 copy-start.1
  0.0 0.0 copy-start.2
  0.0 1.1 slice_bitcast_fusion
  1.1 0.2 copy.9
  1.3 2.4 %copy.8 = bf16[128,8,2,128]{0,2,1,3:T(2,128)(2,1)S(1)} copy(bf16[128,8,2,128]{3,2,1,0:T(2,128)(2,1)} %param.4) | data formatting | bytes 1048576 | tf_op args[0]
  3.7 0.0 copy-done
  3.8 0.0 copy-done.1
  3.8 0.0 copy-done.2
  3.8 131.4 %correlate_pairs.1 = f32[2,8,128,256]{3,2,1,0:T(8,128)S(1)} custom-call(s32[2,64]{1,0:T(2,128)S(1)} %copy-done.2, bf16[128,16,128]{2,1,0:T(8,128)(2,1)S(1)} %bitcast.8, bf16[8,128,128]{2,1,0:T(8,128)(2,1)S(1)} %bitcast.9, bf16[256,2048]{1,0:T(8,128)(2,1)S(1)} %copy-done.1, bf16[128,4096]{1,0:T(8,128)(2,1)S(1)} %copy-done), custom_call_target="tpu_custom_call" | custom-call | tf_op jit(solution)/shard_map/correlate_pairs/pallas_call | solution.py:457
  135.2 1.3 copy.11
Async XLA Ops:
  0.0 3.7 %copy-start = (bf16[128,4096]{1,0:T(8,128)(2,1)S(1)}, bf16[128,4096]{1,0:T(8,128)(2,1)}, u32[]{:S(2)}) copy-start(bf16[128,4096]{1,0:T(8,128)(2,1)} %constant.5.clone.picks) | copy-start | bytes 3145732
  0.0 3.7 %copy-start.1 = (bf16[256,2048]{1,0:T(8,128)(2,1)S(1)}, bf16[256,2048]{1,0:T(8,128)(2,1)}, u32[]{:S(2)}) copy-start(bf16[256,2048]{1,0:T(8,128)(2,1)} %constant.4.clone.table) | copy-start | bytes 3145732
  0.0 3.8 %copy-start.2 = (s32[2,64]{1,0:T(2,128)S(1)}, s32[2,64]{1,0:T(2,128)}, u32[]{:S(2)}) copy-start(s32[2,64]{1,0:T(2,128)} %pair.1) | copy-start | bytes 1540

commit v4 on v3

--- a/solution.py
+++ b/solution.py
@@ -14,7 +14,7 @@
 ROUNDS = 2
 MESH = pl.DeviceIdType.MESH
 PARTS = 4
-BATCH = 4
+BATCH = 8
 Y_FIRST = ((0, 1), (1, 1), (2, 1))
 ORDER = (
     ("E0", "Z1", "P0", "Z2", "E1", "Q0", "E2", "R0", "X0", "P1", "Q1", "R1", "X1", "O0", "E3", "W0")
@@ -262,9 +262,12 @@
 
         lax.fori_loop(1, depth, one, 0)
         own = block(a, r, q)
+        if (a, r) not in Y_FIRST:
+            ship(own, a, r, 0, mate_dev)
         ship(own, a, r, 1, up_dev)
         ship(own, a, r, 3, down_dev)
-        ship(own, a, r, 0, mate_dev)
+        if (a, r) in Y_FIRST:
+            ship(own, a, r, 0, mate_dev)
 
     def second(a, r):
         if (a, r) in Y_FIRST:

time: 137 us -> 136 us (level)
  the two profiles are of different devices: /device:TPU:16 before, /device:TPU:2 now
where the time goes in v4:
time: 136 us
  Pallas kernels  131 us (96%)
  local copies, waits for them, and re-layouts  5.05 us (4%)
    pallas_call x1, Pallas kernels, per_device(): pl.pallas_call(functools.partial(kernel, depth, ring, windows), out_shape...  131 us
    unnamed x8, local copies, waits for them, and re-layouts  3.75 us

profile of v4, /device:TPU:2, one launch (start us, length us, event | category | flops | bytes accessed | tf_op | source)
XLA Modules:
  0.0 135.6 jit_solution(18096697990493753646)
XLA Ops:
  0.0 0.0 copy-start
  0.0 0.0 copy-start.1
  0.0 0.0 copy-start.2
  0.0 1.1 slice_bitcast_fusion
  1.1 0.2 copy.9
  1.3 2.4 %copy.8 = bf16[128,8,2,128]{0,2,1,3:T(2,128)(2,1)S(1)} copy(bf16[128,8,2,128]{3,2,1,0:T(2,128)(2,1)} %param.4) | data formatting | bytes 1048576 | tf_op args[0]
  3.7 0.0 copy-done
  3.8 0.0 copy-done.1
  3.8 0.0 copy-done.2
  3.8 130.5 %correlate_pairs.1 = f32[2,8,128,256]{3,2,1,0:T(8,128)S(1)} custom-call(s32[2,64]{1,0:T(2,128)S(1)} %copy-done.2, bf16[128,16,128]{2,1,0:T(8,128)(2,1)S(1)} %bitcast.8, bf16[8,128,128]{2,1,0:T(8,128)(2,1)S(1)} %bitcast.9, bf16[256,2048]{1,0:T(8,128)(2,1)S(1)} %copy-done.1, bf16[128,4096]{1,0:T(8,128)(2,1)S(1)} %copy-done), custom_call_target="tpu_custom_call" | custom-call | tf_op jit(solution)/shard_map/correlate_pairs/pallas_call | solution.py:460
  134.3 1.3 copy.11
Async XLA Ops:
  0.0 3.7 %copy-start = (bf16[128,4096]{1,0:T(8,128)(2,1)S(1)}, bf16[128,4096]{1,0:T(8,128)(2,1)}, u32[]{:S(2)}) copy-start(bf16[128,4096]{1,0:T(8,128)(2,1)} %constant.5.clone.picks) | copy-start | bytes 3145732
  0.0 3.7 %copy-start.1 = (bf16[256,2048]{1,0:T(8,128)(2,1)S(1)}, bf16[256,2048]{1,0:T(8,128)(2,1)}, u32[]{:S(2)}) copy-start(bf16[256,2048]{1,0:T(8,128)(2,1)} %constant.4.clone.table) | copy-start | bytes 3145732
  0.0 3.8 %copy-start.2 = (s32[2,64]{1,0:T(2,128)S(1)}, s32[2,64]{1,0:T(2,128)}, u32[]{:S(2)}) copy-start(s32[2,64]{1,0:T(2,128)} %pair.1) | copy-start | bytes 1540
